TPU v7x, 512 devices: a whole 4x4x16 slice. The times are simulated.
512 devices in a mesh: pipe: 2 (over core), dp: 16 (over y, x), tensor: 16 (over z).
Axes of the slice: x: 4, y: 4, z: 16, core: 2. Of those that a mesh axis runs over, the one named last changes fastest.
Arguments:
- x_act: bfloat16 [2, 6144, 16384], P('pipe', 'dp', 'tensor'), may hold values from -6 to 6
- grad_z: bfloat16 [2, 6144, 26624], P('pipe', 'dp', 'tensor'), may hold values from -6 to 6
- weight_tiles: bfloat16 [2, 256, 128, 128], P('pipe', 'tensor'), may hold values from -0.5 to 0.5
- tile_rows: int32 [2, 256], P('pipe', 'tensor'), may hold values from 0 to 127, as said below
- tile_cols: int32 [2, 256], P('pipe', 'tensor'), may hold values from 0 to 12
- err_in: float32 [2, 16, 256, 128, 128], P('pipe', 'dp', 'tensor'), may hold values from -0.3 to 0.3
- kept_mask: int32 [2, 16, 256], P('pipe', 'dp', 'tensor'), may hold values 0 or 1
- tile_list: int32 [2, 16, 192], P('pipe', 'dp', 'tensor'), may hold values from 0 to 23, as said below
- live_count: int32 [2, 16, 16], P('pipe', 'dp', 'tensor'), may hold values from 1 to 12, as said below
Outputs:
- recv_tiles: bfloat16 [2, 16, 192, 128, 128], P('pipe', 'dp', 'tensor')
- err_out: float32 [2, 16, 256, 128, 128], P('pipe', 'dp', 'tensor')
- grad_sum: float32 [2, 16, 16, 128, 128], P('pipe', 'dp', 'tensor')
Inputs may be any that keep to these rules, and one draw needn't show every extreme that they name: `tile_rows`: entry j of a tensor rank's 16 entries of one section names a column block held by tensor rank j // (16 / 16), that is one of the blocks ((j // (16 / 16)) * L to that plus L - 1, L = 16384 / (128 * 16)). `tile_list`: A device's 12 entries are distinct tile numbers m * L + b of its own region (L = 16384 / (128 * 16), m < 3, b < L). `live_count`: some device uses all 12 entries of its list.
All inputs are finite; a program needn't handle non-finite values. No bound on the sum of `kept_mask` on one device may be relied on, other than what follows from the above.
Results may differ from a plain program's by a relative error of at most 0.0048.
Values may be sent and summed in bfloat16 or wider, within the bound.
A program may use at most 128 MiB of HBM per device.

v0:
```python
import jax
import jax.numpy as jnp
from jax import lax
from jax.sharding import PartitionSpec as P


def shifted(value, axis, by):
    count = lax.axis_size(axis)
    return lax.ppermute(value, axis, [(i, (i + by) % count) for i in range(count)])


def pack_listed(input_grad, listed, live_now, tile_size, local_blocks):
    tok_count = input_grad.shape[0]
    grid = input_grad.reshape(tok_count // tile_size, tile_size, local_blocks, tile_size)
    picked = grid[listed // local_blocks, :, listed % local_blocks, :]
    valid = jnp.arange(listed.shape[0], dtype=jnp.int32) < live_now[0]
    return jnp.where(valid[:, None, None], picked, jnp.zeros_like(picked))


def local(
    x_act, grad_z, weight_tiles, tile_rows, tile_cols, err_in, kept_mask, tile_list, live_count
):
    tensor_count = lax.axis_size("tensor")
    inputs = x_act[0]
    grads_out = grad_z[0]
    stored = weight_tiles[0]
    row_ids = tile_rows[0]
    col_ids = tile_cols[0]
    tok_count = inputs.shape[0]
    tile_size = stored.shape[1]
    local_blocks = inputs.shape[1] // tile_size
    local_rows = row_ids % local_blocks
    grad_blocks = grads_out.reshape(tok_count, grads_out.shape[1] // tile_size, tile_size)
    grad_sel = jnp.take(grad_blocks, col_ids, axis=1)
    gathered = lax.all_gather(inputs, "tensor", axis=1, tiled=True)
    input_sel = jnp.take(
        gathered.reshape(tok_count, local_blocks * tensor_count, tile_size), row_ids, axis=1
    )
    weight_grads = jnp.einsum(
        "tkc,tkf->kcf", input_sel, grad_sel, preferred_element_type=jnp.float32
    ) * (1.0 / tok_count)
    accumulated = weight_grads + err_in[0, 0]
    keep_now = (kept_mask[0, 0] == 1)[:, None, None]
    sent_tiles = jnp.where(keep_now, accumulated, jnp.float32(0.0))
    residual = accumulated - sent_tiles
    summed = lax.psum_scatter(sent_tiles, "dp", scatter_dimension=0, tiled=True)
    partial_value = jnp.einsum(
        "tkf,kcf->tkc", grad_sel, stored, preferred_element_type=jnp.float32
    ).astype(jnp.bfloat16)
    arrived_terms, arrived_rows = (
        lax.all_to_all(partial_value, "tensor", split_axis=1, concat_axis=1, tiled=True),
        lax.all_to_all(local_rows[None, :], "tensor", split_axis=1, concat_axis=1, tiled=True),
    )
    onehot = (
        arrived_rows[0][:, None] == jnp.arange(local_blocks, dtype=jnp.int32)[None, :]
    ).astype(jnp.bfloat16)
    input_grad = jnp.einsum(
        "trc,rb->tbc", arrived_terms, onehot, preferred_element_type=jnp.float32
    ).astype(jnp.bfloat16)
    listed = tile_list[0, 0]
    live_now = live_count[0, 0]
    grad_in, listed_in, live_in = shifted((input_grad, listed, live_now), "pipe", -1)
    arrived = pack_listed(grad_in, listed_in, live_in, tile_size, local_blocks)
    return (arrived[None, None], residual[None, None], summed[None, None])


def solution(mesh):
    return jax.shard_map(
        local,
        mesh=mesh,
        in_specs=(
            P("pipe", "dp", "tensor"),
            P("pipe", "dp", "tensor"),
            P("pipe", "tensor", None, None),
            P("pipe", "tensor"),
            P("pipe", "tensor"),
            P("pipe", "dp", "tensor", None, None),
            P("pipe", "dp", "tensor"),
            P("pipe", "dp", "tensor"),
            P("pipe", "dp", "tensor"),
        ),
        out_specs=(
            P("pipe", "dp", "tensor", None, None),
            P("pipe", "dp", "tensor", None, None),
            P("pipe", "dp", "tensor", None, None),
        ),
        check_vma=False,
    )
```

profile of v0, /device:TPU:2, one launch (start us, length us, event | category | flops | bytes accessed | tf_op | source)
XLA Modules:
  0.0 350.0 jit_solution(13440303011730557698)
XLA Ops:
  7.2 0.0 copy-start
  7.2 0.0 copy-start.5
  7.2 0.0 copy-start.2
  7.2 0.0 all-gather.3.cloned.1.call-start
  7.2 2.4 copy.37
  9.7 0.0 all-gather.3.cloned.1.call-update
  9.7 0.0 copy-done.5
  9.7 0.7 copy.32
  10.4 15.2 %all-to-all-start = ((s32[1,16,1]{2,0,1:T(1,128)}), s32[1,16,1]{2,0,1:T(1,128)S(1)}, u32[]{:S(2)}, u32[]{:S(2)}) async-start(s32[1,16,1]{2,0,1:T(1,128)} %copy.32), calls=%async_computation | async-start | bytes 16384 | tf_op jit(solution)/shard_map/all_to_all | solution.py:52
  25.6 0.0 copy-done.2
  25.6 1.7 copy.33
  27.3 0.0 copy-start.4
  27.3 2.1 copy.34
  29.4 0.0 copy-done.4
  29.4 0.9 gather_fusion
  30.3 0.0 copy-start.1
  30.3 0.0 copy-done
  30.3 1.8 fusion.8
  32.1 0.0 copy-done.1
  32.1 0.0 copy-start.6
  32.1 5.8 %all-to-all-done = s32[1,16,1]{2,0,1:T(1,128)S(1)} async-done(((s32[1,16,1]{2,0,1:T(1,128)}), s32[1,16,1]{2,0,1:T(1,128)S(1)}, u32[]{:S(2)}, u32[]{:S(2)}) %all-to-all-start) | async-done | bytes 96 | tf_op jit(solution)/shard_map/all_to_all | solution.py:52
  38.0 6.3 %all-to-all-start.1 = ((bf16[384,16,128]{2,0,1:T(8,128)(2,1)}), bf16[384,16,128]{2,0,1:T(8,128)(2,1)S(1)}, u32[]{:S(2)}, u32[]{:S(2)}) async-start(bf16[384,16,128]{2,0,1:T(8,128)(2,1)} %fusion.8), calls=%async_computation.1 | async-start | bytes 3145728 | tf_op jit(solution)/shard_map/all_to_all | solution.py:51
  44.3 0.0 reduce-scatter.4.cloned.1.call-start
  44.4 0.0 copy-done.6
  44.4 186.3 %all-gather.3.cloned.1.call-done = bf16[1,384,16384]{1,2,0:T(8,128)(2,1)} async-done(((bf16[1,384,1024]{1,2,0:T(8,128)(2,1)}), bf16[1,384,16384]{1,2,0:T(8,128)(2,1)}) %all-gather.3.cloned.1.call-update) | async-done | bytes 12582928 | tf_op jit(solution)/shard_map/all_gather | solution.py:35
  230.7 15.8 %copy.38 = bf16[384,128,128]{2,0,1:T(8,128)(2,1)} copy(bf16[384,128,128]{0,2,1:T(8,128)(2,1)} %bitcast.64) | data formatting | bytes 25165824 | tf_op jit(solution)/shard_map/reshape | solution.py:37
  246.5 0.0 copy-start.3
  246.5 6.6 %gather_fusion.2 = bf16[16,384,128]{2,1,0:T(8,128)(2,1)} fusion(bf16[384,128,128]{2,0,1:T(8,128)(2,1)} %copy.38, s32[1024]{0:T(1024)S(1)} %pad_clamp_fusion), kind=kCustom, calls=%fused_computation.2 | custom fusion | bytes 3145792 | tf_op jit(solution)/shard_map/jit(_take)/gather | solution.py:36
  253.1 0.0 copy-done.3
  253.1 4.1 %broadcast_select_fusion.3 = (f32[16,128,128]{2,1,0:T(8,128)}, f32[1,1,16,128,128]{4,3,2,1,0:T(8,128)}) fusion(pred[16]{0:T(512)(128)(4,1)S(1)} %compare_bitcast_fusion, f32[1,1,16,128,128]{4,3,2,1,0:T(8,128)S(1)} %copy-done.3, bf16[16,384,128]{2,1,0:T(8,128)(2,1)} %copy-done.1, pred[16]{0:T(512)(128)(4,1)S(1)} %compare_and_fusion.1, ...), kind=kOutput, calls=%fused_computation.21 | convolution fusion | flops 203948032 | bytes 6291504 | tf_op jit(solution)/shard_map/tkc,tkf->kcf/dot_general | solution.py:39
  257.2 0.0 copy-start.7
  257.2 0.0 reduce-scatter.4.cloned.1.call-update
  257.2 0.4 reduce
  257.6 0.0 all-to-all-done.1
  257.6 0.9 fusion.24
  258.6 1.9 collective-permute-start.1
  260.5 0.0 copy-done.7
  260.5 2.4 collective-permute-start.2
  262.9 1.9 collective-permute-start
  264.9 1.4 collective-permute-done
  266.2 0.6 iota_compare_fusion.1
  266.9 0.0 collective-permute-done.2
  266.9 0.0 collective-permute-done.1
  266.9 0.2 copy.36
  267.1 0.7 gather_fusion.1
  267.8 0.8 bitcast_select_fusion
  268.6 74.6 %reduce-scatter.4.cloned.1.call-done = f32[1,128,128]{2,1,0:T(8,128)} async-done(((f32[16,128,128]{2,1,0:T(8,128)}), f32[1,128,128]{2,1,0:T(8,128)}) %reduce-scatter.4.cloned.1.call-update) | async-done | bytes 65552
  (9 shorter events, 0.1 us)
Async XLA Ops:
  7.2 23.1 %copy-start = (bf16[1,16,128,128]{3,2,1,0:T(8,128)(2,1)S(1)}, bf16[1,16,128,128]{3,2,1,0:T(8,128)(2,1)}, u32[]{:S(2)}) copy-start(bf16[1,16,128,128]{3,2,1,0:T(8,128)(2,1)} %param.11) | copy-start | bytes 1572868
  7.2 2.5 copy-start.5
  7.2 18.4 %copy-start.2 = (bf16[1,384,1664]{2,1,0:T(8,128)(2,1)S(1)}, bf16[1,384,1664]{2,1,0:T(8,128)(2,1)}, u32[]{:S(2)}) copy-start(bf16[1,384,1664]{2,1,0:T(8,128)(2,1)} %param.10) | copy-start | bytes 3833860
  7.2 223.5 %all-gather.3.cloned.1.call-start = ((), (), s32[]{:S(2)}) async-start(), calls=%async_computation.3 | async-start | bytes 13369344 | tf_op jit(solution)/shard_map/all_gather | solution.py:35
  10.4 27.6 %all-to-all-start = ((s32[1,16,1]{2,0,1:T(1,128)}), s32[1,16,1]{2,0,1:T(1,128)S(1)}, u32[]{:S(2)}, u32[]{:S(2)}) async-start(s32[1,16,1]{2,0,1:T(1,128)} %copy.32), calls=%async_computation | async-start | bytes 16384 | tf_op jit(solution)/shard_map/all_to_all | solution.py:52
  27.3 2.1 copy-start.4
  30.3 1.9 copy-start.1
  32.1 12.3 %copy-start.6 = (s32[1,1,16]{2,1,0:T(1,128)S(1)}, s32[1,1,16]{2,1,0:T(1,128)}, u32[]{:S(2)}) copy-start(s32[1,1,16]{2,1,0:T(1,128)} %param.15) | copy-start | bytes 196
  38.0 219.7 %all-to-all-start.1 = ((bf16[384,16,128]{2,0,1:T(8,128)(2,1)}), bf16[384,16,128]{2,0,1:T(8,128)(2,1)S(1)}, u32[]{:S(2)}, u32[]{:S(2)}) async-start(bf16[384,16,128]{2,0,1:T(8,128)(2,1)} %fusion.8), calls=%async_computation.1 | async-start | bytes 3145728 | tf_op jit(solution)/shard_map/all_to_all | solution.py:51
  44.3 298.9 %reduce-scatter.4.cloned.1.call-start = ((), (), s32[]{:S(2)}) async-start(), calls=%async_computation.4 | async-start | bytes 1114112
  246.5 6.6 %copy-start.3 = (f32[1,1,16,128,128]{4,3,2,1,0:T(8,128)S(1)}, f32[1,1,16,128,128]{4,3,2,1,0:T(8,128)}, u32[]{:S(2)}) copy-start(f32[1,1,16,128,128]{4,3,2,1,0:T(8,128)} %param.14) | copy-start | bytes 3145732
  257.2 3.3 copy-start.7
  258.6 8.3 %collective-permute-start.1 = (bf16[384,8,128]{2,1,0:T(8,128)(2,1)S(1)}, bf16[384,8,128]{2,1,0:T(8,128)(2,1)S(1)}, u32[]{:S(2)}, u32[]{:S(2)}) collective-permute-start(bf16[384,8,128]{2,1,0:T(8,128)(2,1)S(1)} %fusion.24), channel_id=1, source_target_pairs={{0,256},{256,0},{1,257},{257,1},{2,258},{258,2},{3,259},{259,3},{4... | collective-permute-start | bytes 2359304 | tf_op jit(solution)/shard_map/ppermute | solution.py:9
  260.5 6.3 %collective-permute-start.2 = (s32[12]{0:T(128)S(1)}, s32[12]{0:T(128)S(1)}, u32[]{:S(2)}, u32[]{:S(2)}) collective-permute-start(s32[12]{0:T(128)S(1)} %bitcast.68), channel_id=1, source_target_pairs={{0,256},{256,0},{1,257},{257,1},{2,258},{258,2},{3,259},{259,3},{4... | collective-permute-start | bytes 152 | tf_op jit(solution)/shard_map/ppermute | solution.py:9
  262.9 3.3 collective-permute-start
Sparse Core Ops, SparseCore 0:
  10.7 219.9 all-gather.2
  257.4 85.7 reduce-scatter.3
where the time goes:
time: 351 us; the launch traced here: 350 us
  waiting for transfers between devices  268 us (76%)
  local copies, waits for them, and re-layouts  31 us (9%)
  starting transfers between devices  27.9 us (8%)
  between operations  14.3 us (4%)
  matrix products  6.86 us (2%)
    all_gather x1, waiting for transfers between devices, local(): gathered = lax.all_gather(inputs, 'tensor', axis=1, tiled=True)  186 us
    unnamed x3, waiting for transfers between devices  74.6 us
    reshape x1, local copies, waits for them, and re-layouts, local(): gathered.reshape(tok_count, local_blocks * tensor_count, tile_size)  15.8 us
    all_to_all x1, starting transfers between devices, local(): lax.all_to_all(local_rows[None, :], 'tensor', split_axis=1, concat_axis=1...  15.2 us
  transfers between devices with their start and end apart: 7, of which 4 were waited for; matrix products, arithmetic and copies ran while one was open for 11% of the time, Pallas kernels for 0%

commit v1 on v0

--- a/solution.py
+++ b/solution.py
@@ -32,7 +32,17 @@
     local_rows = row_ids % local_blocks
     grad_blocks = grads_out.reshape(tok_count, grads_out.shape[1] // tile_size, tile_size)
     grad_sel = jnp.take(grad_blocks, col_ids, axis=1)
-    gathered = lax.all_gather(inputs, "tensor", axis=1, tiled=True)
+    total_devices = lax.axis_size("tensor")
+    line_up = [inputs]
+    for c in [*range(total_devices - 1)]:
+        line_up.append(
+            lax.ppermute(
+                line_up[-1], "tensor", [(m, (m + 1) % total_devices) for m in range(total_devices)]
+            )
+        )
+    gathered = jnp.roll(
+        jnp.concatenate(line_up[::-1], 1), (lax.axis_index("tensor") + 1) * inputs.shape[1], 1
+    )
     input_sel = jnp.take(
         gathered.reshape(tok_count, local_blocks * tensor_count, tile_size), row_ids, axis=1
     )

time: 351 us -> 525 us (1.50)
  local copies, waits for them, and re-layouts: 31 us -> 117 us
  waiting for transfers between devices: 268 us -> 319 us
  starting transfers between devices: 27.9 us -> 57.1 us
    ppermute x0 -> x15, waiting for transfers between devices: none -> 240 us  [local(): lax.ppermute(line_up[-1], 'tensor', [(m, (m + 1) % total_devices) for m i...]
    all_gather x1 -> x0, waiting for transfers between devices: 186 us -> none  [local(): gathered = lax.all_gather(inputs, 'tensor', axis=1, tiled=True)]
    unnamed x18 -> x65, local copies, waits for them, and re-layouts: 4.14 us -> 77 us
    ppermute x0 -> x15, starting transfers between devices: none -> 30.5 us  [local(): lax.ppermute(line_up[-1], 'tensor', [(m, (m + 1) % total_devices) for m i...]
    dynamic_slice x0 -> x1, local copies, waits for them, and re-layouts: none -> 10.6 us  [local(): jnp.roll(jnp.concatenate(line_up[::-1], 1), (lax.axis_index('tensor') + 1...]
    all_to_all x1, waiting for transfers between devices: 5.83 us -> 0.01 us  [local(): lax.all_to_all(local_rows[None, :], 'tensor', split_axis=1, concat_axis=1...]
    unnamed x3 -> x2, waiting for transfers between devices: 74.6 us -> 78.1 us
  transfers between devices with their start and end apart: 7 -> 21, of which waited for: 4 -> 17; matrix products, arithmetic and copies ran while one was open for 11% -> 23% of each run, Pallas kernels for 0% -> 0%
where the time goes in v1:
time: 525 us; the launch traced here: 523 us
  waiting for transfers between devices  319 us (61%)
  local copies, waits for them, and re-layouts  117 us (22%)
  starting transfers between devices  57.1 us (11%)
  between operations  14.3 us (3%)
  matrix products  8.48 us (2%)
  other arithmetic  5.91 us (1%)
    ppermute x15, waiting for transfers between devices, local(): lax.ppermute(line_up[-1], 'tensor', [(m, (m + 1) % total_devices) for m i...  240 us
    unnamed x2, waiting for transfers between devices  78.1 us
    unnamed x65, local copies, waits for them, and re-layouts  77 us
    ppermute x15, starting transfers between devices, local(): lax.ppermute(line_up[-1], 'tensor', [(m, (m + 1) % total_devices) for m i...  30.5 us
    reshape x1, local copies, waits for them, and re-layouts, local(): gathered.reshape(tok_count, local_blocks * tensor_count, tile_size)  16.7 us
    dynamic_slice x1, local copies, waits for them, and re-layouts, local(): jnp.roll(jnp.concatenate(line_up[::-1], 1), (lax.axis_index('tensor') + 1...  10.6 us
  transfers between devices with their start and end apart: 21, of which 17 were waited for; matrix products, arithmetic and copies ran while one was open for 23% of the time, Pallas kernels for 0%

profile of v1, /device:TPU:2, one launch (start us, length us, event | category | flops | bytes accessed | tf_op | source)
XLA Modules:
  0.0 522.6 jit_solution(13769994064153454400)
XLA Ops:
  8.7 3.8 collective-permute-start.3
  12.6 25.1 %collective-permute-done.3 = bf16[384,1024]{0,1:T(8,128)(2,1)S(1)} collective-permute-done((bf16[384,1024]{0,1:T(8,128)(2,1)S(1)}, bf16[384,1024]{0,1:T(8,128)(2,1)S(1)}, u32[]{:S(2)}, u32[]{:S(2)}) %collective-permute-start.3) | collective-permute-done | bytes 786464 | tf_op jit(solution)/shard_map/ppermute | solution.py:39
  40.5 19.9 %collective-permute-done.4 = bf16[384,1024]{0,1:T(8,128)(2,1)S(1)} collective-permute-done((bf16[384,1024]{0,1:T(8,128)(2,1)S(1)}, bf16[384,1024]{0,1:T(8,128)(2,1)S(1)}, u32[]{:S(2)}, u32[]{:S(2)}) %collective-permute-start.4) | collective-permute-done | bytes 786464 | tf_op jit(solution)/shard_map/ppermute | solution.py:39
  62.3 19.0 %collective-permute-done.5 = bf16[384,1024]{0,1:T(8,128)(2,1)S(1)} collective-permute-done((bf16[384,1024]{0,1:T(8,128)(2,1)S(1)}, bf16[384,1024]{0,1:T(8,128)(2,1)S(1)}, u32[]{:S(2)}, u32[]{:S(2)}) %collective-permute-start.5) | collective-permute-done | bytes 786464 | tf_op jit(solution)/shard_map/ppermute | solution.py:39
  84.1 18.1 %collective-permute-done.6 = bf16[384,1024]{0,1:T(8,128)(2,1)S(1)} collective-permute-done((bf16[384,1024]{0,1:T(8,128)(2,1)S(1)}, bf16[384,1024]{0,1:T(8,128)(2,1)S(1)}, u32[]{:S(2)}, u32[]{:S(2)}) %collective-permute-start.6) | collective-permute-done | bytes 786464 | tf_op jit(solution)/shard_map/ppermute | solution.py:39
  105.0 17.1 %collective-permute-done.7 = bf16[384,1024]{0,1:T(8,128)(2,1)S(1)} collective-permute-done((bf16[384,1024]{0,1:T(8,128)(2,1)S(1)}, bf16[384,1024]{0,1:T(8,128)(2,1)S(1)}, u32[]{:S(2)}, u32[]{:S(2)}) %collective-permute-start.7) | collective-permute-done | bytes 786464 | tf_op jit(solution)/shard_map/ppermute | solution.py:39
  124.9 16.2 %collective-permute-done.8 = bf16[384,1024]{0,1:T(8,128)(2,1)S(1)} collective-permute-done((bf16[384,1024]{0,1:T(8,128)(2,1)S(1)}, bf16[384,1024]{0,1:T(8,128)(2,1)S(1)}, u32[]{:S(2)}, u32[]{:S(2)}) %collective-permute-start.8) | collective-permute-done | bytes 786464 | tf_op jit(solution)/shard_map/ppermute | solution.py:39
  144.0 15.3 %collective-permute-done.9 = bf16[384,1024]{0,1:T(8,128)(2,1)S(1)} collective-permute-done((bf16[384,1024]{0,1:T(8,128)(2,1)S(1)}, bf16[384,1024]{0,1:T(8,128)(2,1)S(1)}, u32[]{:S(2)}, u32[]{:S(2)}) %collective-permute-start.9) | collective-permute-done | bytes 786464 | tf_op jit(solution)/shard_map/ppermute | solution.py:39
  162.1 14.9 %collective-permute-done.10 = bf16[384,1024]{0,1:T(8,128)(2,1)S(1)} collective-permute-done((bf16[384,1024]{0,1:T(8,128)(2,1)S(1)}, bf16[384,1024]{0,1:T(8,128)(2,1)S(1)}, u32[]{:S(2)}, u32[]{:S(2)}) %collective-permute-start.10) | collective-permute-done | bytes 786464 | tf_op jit(solution)/shard_map/ppermute | solution.py:39
  179.8 14.9 %collective-permute-done.11 = bf16[384,1024]{0,1:T(8,128)(2,1)S(1)} collective-permute-done((bf16[384,1024]{0,1:T(8,128)(2,1)S(1)}, bf16[384,1024]{0,1:T(8,128)(2,1)S(1)}, u32[]{:S(2)}, u32[]{:S(2)}) %collective-permute-start.11) | collective-permute-done | bytes 786464 | tf_op jit(solution)/shard_map/ppermute | solution.py:39
  197.5 15.6 %collective-permute-done.12 = bf16[384,1024]{0,1:T(8,128)(2,1)S(1)} collective-permute-done((bf16[384,1024]{0,1:T(8,128)(2,1)S(1)}, bf16[384,1024]{0,1:T(8,128)(2,1)S(1)}, u32[]{:S(2)}, u32[]{:S(2)}) %collective-permute-start.12) | collective-permute-done | bytes 786464 | tf_op jit(solution)/shard_map/ppermute | solution.py:39
  216.0 16.7 %collective-permute-done.13 = bf16[384,1024]{0,1:T(8,128)(2,1)S(1)} collective-permute-done((bf16[384,1024]{0,1:T(8,128)(2,1)S(1)}, bf16[384,1024]{0,1:T(8,128)(2,1)S(1)}, u32[]{:S(2)}, u32[]{:S(2)}) %collective-permute-start.13) | collective-permute-done | bytes 786464 | tf_op jit(solution)/shard_map/ppermute | solution.py:39
  235.5 17.8 %collective-permute-done.14 = bf16[384,1024]{0,1:T(8,128)(2,1)S(1)} collective-permute-done((bf16[384,1024]{0,1:T(8,128)(2,1)S(1)}, bf16[384,1024]{0,1:T(8,128)(2,1)S(1)}, u32[]{:S(2)}, u32[]{:S(2)}) %collective-permute-start.14) | collective-permute-done | bytes 786464 | tf_op jit(solution)/shard_map/ppermute | solution.py:39
  256.1 19.8 %collective-permute-done.15 = bf16[384,1024]{0,1:T(8,128)(2,1)S(1)} collective-permute-done((bf16[384,1024]{0,1:T(8,128)(2,1)S(1)}, bf16[384,1024]{0,1:T(8,128)(2,1)S(1)}, u32[]{:S(2)}, u32[]{:S(2)}) %collective-permute-start.15) | collective-permute-done | bytes 786464 | tf_op jit(solution)/shard_map/ppermute | solution.py:39
  279.1 10.0 %all-to-all-start = ((s32[1,16,1]{2,0,1:T(1,128)}), s32[1,16,1]{2,0,1:T(1,128)S(1)}, u32[]{:S(2)}, u32[]{:S(2)}) async-start(s32[1,16,1]{2,0,1:T(1,128)} %copy.32), calls=%async_computation | async-start | bytes 16384 | tf_op jit(solution)/shard_map/all_to_all | solution.py:62
  291.1 7.4 %collective-permute-done.16 = bf16[384,1024]{0,1:T(8,128)(2,1)} collective-permute-done((bf16[384,1024]{0,1:T(8,128)(2,1)S(1)}, bf16[384,1024]{0,1:T(8,128)(2,1)}, u32[]{:S(2)}, u32[]{:S(2)}) %collective-permute-start.16) | collective-permute-done | bytes 786464 | tf_op jit(solution)/shard_map/ppermute | solution.py:39
  300.4 2.5 copy.33
  303.0 2.2 copy.34
  308.4 3.2 fusion.8
  311.6 2.4 collective-permute-done.17
  313.9 2.1 constant_dynamic-update-slice_fusion.31
  316.0 2.1 constant_dynamic-update-slice_fusion.30
  318.1 2.1 constant_dynamic-update-slice_fusion.29
  324.4 2.1 constant_dynamic-update-slice_fusion.26
  326.5 2.1 constant_dynamic-update-slice_fusion.25
  328.6 2.1 constant_dynamic-update-slice_fusion.24
  330.8 2.1 constant_dynamic-update-slice_fusion.23
  332.8 2.1 constant_dynamic-update-slice_fusion.22
  335.0 2.1 constant_dynamic-update-slice_fusion.21
  339.2 2.1 constant_dynamic-update-slice_fusion.19
  342.3 10.3 %all-to-all-start.1 = ((bf16[384,16,128]{2,0,1:T(8,128)(2,1)}), bf16[384,16,128]{2,0,1:T(8,128)(2,1)S(1)}, u32[]{:S(2)}, u32[]{:S(2)}) async-start(bf16[384,16,128]{2,0,1:T(8,128)(2,1)} %fusion.8), calls=%async_computation.1 | async-start | bytes 3145728 | tf_op jit(solution)/shard_map/all_to_all | solution.py:61
  355.7 2.1 constant_dynamic-update-slice_fusion.15
  359.9 2.1 constant_dynamic-update-slice_fusion.13
  362.0 2.1 constant_dynamic-update-slice_fusion.12
  364.1 2.1 constant_dynamic-update-slice_fusion.11
  368.3 2.1 constant_dynamic-update-slice_fusion.9
  372.5 2.1 constant_dynamic-update-slice_fusion.7
  374.6 2.1 constant_dynamic-update-slice_fusion.6
  378.8 2.1 constant_dynamic-update-slice_fusion.4
  380.9 2.1 constant_dynamic-update-slice_fusion.3
  383.0 2.1 constant_dynamic-update-slice_fusion.2
  385.2 2.1 constant_dynamic-update-slice_fusion.1
  388.3 10.6 %constant_dynamic-slice_fusion = bf16[384,16384]{0,1:T(8,128)(2,1)} fusion(bf16[384,32768]{0,1:T(8,128)(2,1)} %constant_dynamic-update-slice_fusion, s32[]{:T(128)S(6)} %select_n.102), kind=kLoop, calls=%fused_computation.87 | loop fusion | bytes 25165828 | tf_op jit(solution)/shard_map/jit(_roll_dynamic)/dynamic_slice | solution.py:43
  398.9 16.7 %copy.38 = bf16[384,128,128]{2,0,1:T(8,128)(2,1)} copy(bf16[384,128,128]{0,2,1:T(8,128)(2,1)} %bitcast.67) | data formatting | bytes 25165824 | tf_op jit(solution)/shard_map/reshape | solution.py:47
  415.6 6.5 %gather_fusion.2 = bf16[16,384,128]{2,1,0:T(8,128)(2,1)} fusion(bf16[384,128,128]{2,0,1:T(8,128)(2,1)} %copy.38, s32[1024]{0:T(1024)S(1)} %pad_clamp_fusion), kind=kCustom, calls=%fused_computation.2 | custom fusion | bytes 3145792 | tf_op jit(solution)/shard_map/jit(_take)/gather | solution.py:46
  422.0 4.4 broadcast_select_fusion.3
  429.7 2.4 collective-permute-start.2
  437.7 78.1 %reduce-scatter.4.cloned.1.call-done = f32[1,128,128]{2,1,0:T(8,128)} async-done(((f32[16,128,128]{2,1,0:T(8,128)}), f32[1,128,128]{2,1,0:T(8,128)}) %reduce-scatter.4.cloned.1.call-update) | async-done | bytes 65552
  (84 shorter events, 73.2 us)
Async XLA Ops:
  7.2 301.2 %copy-start = (bf16[1,16,128,128]{3,2,1,0:T(8,128)(2,1)S(1)}, bf16[1,16,128,128]{3,2,1,0:T(8,128)(2,1)}, u32[]{:S(2)}) copy-start(bf16[1,16,128,128]{3,2,1,0:T(8,128)(2,1)} %param.11) | copy-start | bytes 1572868
  8.7 28.9 %collective-permute-start.3 = (bf16[384,1024]{0,1:T(8,128)(2,1)S(1)}, bf16[384,1024]{0,1:T(8,128)(2,1)S(1)}, u32[]{:S(2)}, u32[]{:S(2)}) collective-permute-start(bf16[384,1024]{0,1:T(8,128)(2,1)S(1)} %bitcast.68), channel_id=1, source_target_pairs={{0,1},{1,2},{2,3},{3,4},{4,5},{5,6},{6,7},{7,8},{8,9},{9,10},{10,1... | collective-permute-start | bytes 2359304 | tf_op jit(solution)/shard_map/ppermute | solution.py:39
  37.7 0.9 copy-start.2
  38.6 21.8 %collective-permute-start.4 = (bf16[384,1024]{0,1:T(8,128)(2,1)S(1)}, bf16[384,1024]{0,1:T(8,128)(2,1)S(1)}, u32[]{:S(2)}, u32[]{:S(2)}) collective-permute-start(bf16[384,1024]{0,1:T(8,128)(2,1)S(1)} %collective-permute-done.3), channel_id=1, source_target_pairs={{0,1},{1,2},{2,3},{3,4},{4,5},{5,6},{6,7},{7,8},{8,9},{9,10},{10,1... | collective-permute-start | bytes 2359304 | tf_op jit(solution)/shard_map/ppermute | solution.py:39
  60.4 281.9 %copy-start.3 = (bf16[384,1024]{0,1:T(8,128)(2,1)}, bf16[384,1024]{0,1:T(8,128)(2,1)S(1)}, u32[]{:S(2)}) copy-start(bf16[384,1024]{0,1:T(8,128)(2,1)S(1)} %collective-permute-done.4) | copy-start | bytes 2359300
  60.4 20.9 %collective-permute-start.5 = (bf16[384,1024]{0,1:T(8,128)(2,1)S(1)}, bf16[384,1024]{0,1:T(8,128)(2,1)S(1)}, u32[]{:S(2)}, u32[]{:S(2)}) collective-permute-start(bf16[384,1024]{0,1:T(8,128)(2,1)S(1)} %collective-permute-done.4), channel_id=1, source_target_pairs={{0,1},{1,2},{2,3},{3,4},{4,5},{5,6},{6,7},{7,8},{8,9},{9,10},{10,1... | collective-permute-start | bytes 2359304 | tf_op jit(solution)/shard_map/ppermute | solution.py:39
  81.3 0.9 copy-start.4
  82.2 20.0 %collective-permute-start.6 = (bf16[384,1024]{0,1:T(8,128)(2,1)S(1)}, bf16[384,1024]{0,1:T(8,128)(2,1)S(1)}, u32[]{:S(2)}, u32[]{:S(2)}) collective-permute-start(bf16[384,1024]{0,1:T(8,128)(2,1)S(1)} %collective-permute-done.5), channel_id=1, source_target_pairs={{0,1},{1,2},{2,3},{3,4},{4,5},{5,6},{6,7},{7,8},{8,9},{9,10},{10,1... | collective-permute-start | bytes 2359304 | tf_op jit(solution)/shard_map/ppermute | solution.py:39
  102.2 0.9 copy-start.5
  103.1 19.1 %collective-permute-start.7 = (bf16[384,1024]{0,1:T(8,128)(2,1)S(1)}, bf16[384,1024]{0,1:T(8,128)(2,1)S(1)}, u32[]{:S(2)}, u32[]{:S(2)}) collective-permute-start(bf16[384,1024]{0,1:T(8,128)(2,1)S(1)} %collective-permute-done.6), channel_id=1, source_target_pairs={{0,1},{1,2},{2,3},{3,4},{4,5},{5,6},{6,7},{7,8},{8,9},{9,10},{10,1... | collective-permute-start | bytes 2359304 | tf_op jit(solution)/shard_map/ppermute | solution.py:39
  122.1 0.9 copy-start.6
  123.0 18.1 %collective-permute-start.8 = (bf16[384,1024]{0,1:T(8,128)(2,1)S(1)}, bf16[384,1024]{0,1:T(8,128)(2,1)S(1)}, u32[]{:S(2)}, u32[]{:S(2)}) collective-permute-start(bf16[384,1024]{0,1:T(8,128)(2,1)S(1)} %collective-permute-done.7), channel_id=1, source_target_pairs={{0,1},{1,2},{2,3},{3,4},{4,5},{5,6},{6,7},{7,8},{8,9},{9,10},{10,1... | collective-permute-start | bytes 2359304 | tf_op jit(solution)/shard_map/ppermute | solution.py:39
  141.1 0.9 copy-start.7
  142.1 17.2 %collective-permute-start.9 = (bf16[384,1024]{0,1:T(8,128)(2,1)S(1)}, bf16[384,1024]{0,1:T(8,128)(2,1)S(1)}, u32[]{:S(2)}, u32[]{:S(2)}) collective-permute-start(bf16[384,1024]{0,1:T(8,128)(2,1)S(1)} %collective-permute-done.8), channel_id=1, source_target_pairs={{0,1},{1,2},{2,3},{3,4},{4,5},{5,6},{6,7},{7,8},{8,9},{9,10},{10,1... | collective-permute-start | bytes 2359304 | tf_op jit(solution)/shard_map/ppermute | solution.py:39
  159.3 0.9 copy-start.8
  160.2 16.8 %collective-permute-start.10 = (bf16[384,1024]{0,1:T(8,128)(2,1)S(1)}, bf16[384,1024]{0,1:T(8,128)(2,1)S(1)}, u32[]{:S(2)}, u32[]{:S(2)}) collective-permute-start(bf16[384,1024]{0,1:T(8,128)(2,1)S(1)} %collective-permute-done.9), channel_id=1, source_target_pairs={{0,1},{1,2},{2,3},{3,4},{4,5},{5,6},{6,7},{7,8},{8,9},{9,10},{10,1... | collective-permute-start | bytes 2359304 | tf_op jit(solution)/shard_map/ppermute | solution.py:39
  177.0 0.9 copy-start.9
  177.9 16.8 %collective-permute-start.11 = (bf16[384,1024]{0,1:T(8,128)(2,1)S(1)}, bf16[384,1024]{0,1:T(8,128)(2,1)S(1)}, u32[]{:S(2)}, u32[]{:S(2)}) collective-permute-start(bf16[384,1024]{0,1:T(8,128)(2,1)S(1)} %collective-permute-done.10), channel_id=1, source_target_pairs={{0,1},{1,2},{2,3},{3,4},{4,5},{5,6},{6,7},{7,8},{8,9},{9,10},{10,1... | collective-permute-start | bytes 2359304 | tf_op jit(solution)/shard_map/ppermute | solution.py:39
  194.7 0.9 copy-start.10
  195.6 17.5 %collective-permute-start.12 = (bf16[384,1024]{0,1:T(8,128)(2,1)S(1)}, bf16[384,1024]{0,1:T(8,128)(2,1)S(1)}, u32[]{:S(2)}, u32[]{:S(2)}) collective-permute-start(bf16[384,1024]{0,1:T(8,128)(2,1)S(1)} %collective-permute-done.11), channel_id=1, source_target_pairs={{0,1},{1,2},{2,3},{3,4},{4,5},{5,6},{6,7},{7,8},{8,9},{9,10},{10,1... | collective-permute-start | bytes 2359304 | tf_op jit(solution)/shard_map/ppermute | solution.py:39
  213.1 0.9 copy-start.11
  214.0 18.6 %collective-permute-start.13 = (bf16[384,1024]{0,1:T(8,128)(2,1)S(1)}, bf16[384,1024]{0,1:T(8,128)(2,1)S(1)}, u32[]{:S(2)}, u32[]{:S(2)}) collective-permute-start(bf16[384,1024]{0,1:T(8,128)(2,1)S(1)} %collective-permute-done.12), channel_id=1, source_target_pairs={{0,1},{1,2},{2,3},{3,4},{4,5},{5,6},{6,7},{7,8},{8,9},{9,10},{10,1... | collective-permute-start | bytes 2359304 | tf_op jit(solution)/shard_map/ppermute | solution.py:39
  232.7 0.9 copy-start.12
  233.5 19.7 %collective-permute-start.14 = (bf16[384,1024]{0,1:T(8,128)(2,1)S(1)}, bf16[384,1024]{0,1:T(8,128)(2,1)S(1)}, u32[]{:S(2)}, u32[]{:S(2)}) collective-permute-start(bf16[384,1024]{0,1:T(8,128)(2,1)S(1)} %collective-permute-done.13), channel_id=1, source_target_pairs={{0,1},{1,2},{2,3},{3,4},{4,5},{5,6},{6,7},{7,8},{8,9},{9,10},{10,1... | collective-permute-start | bytes 2359304 | tf_op jit(solution)/shard_map/ppermute | solution.py:39
  253.3 0.9 copy-start.13
  254.1 21.7 %collective-permute-start.15 = (bf16[384,1024]{0,1:T(8,128)(2,1)S(1)}, bf16[384,1024]{0,1:T(8,128)(2,1)S(1)}, u32[]{:S(2)}, u32[]{:S(2)}) collective-permute-start(bf16[384,1024]{0,1:T(8,128)(2,1)S(1)} %collective-permute-done.14), channel_id=1, source_target_pairs={{0,1},{1,2},{2,3},{3,4},{4,5},{5,6},{6,7},{7,8},{8,9},{9,10},{10,1... | collective-permute-start | bytes 2359304 | tf_op jit(solution)/shard_map/ppermute | solution.py:39
  275.8 27.1 %copy-start.14 = (bf16[384,1024]{0,1:T(8,128)(2,1)}, bf16[384,1024]{0,1:T(8,128)(2,1)S(1)}, u32[]{:S(2)}) copy-start(bf16[384,1024]{0,1:T(8,128)(2,1)S(1)} %collective-permute-done.15) | copy-start | bytes 2359300
  275.9 22.6 %collective-permute-start.16 = (bf16[384,1024]{0,1:T(8,128)(2,1)S(1)}, bf16[384,1024]{0,1:T(8,128)(2,1)}, u32[]{:S(2)}, u32[]{:S(2)}) collective-permute-start(bf16[384,1024]{0,1:T(8,128)(2,1)S(1)} %collective-permute-done.15), channel_id=1, source_target_pairs={{0,1},{1,2},{2,3},{3,4},{4,5},{5,6},{6,7},{7,8},{8,9},{9,10},{10,1... | collective-permute-start | bytes 2359304 | tf_op jit(solution)/shard_map/ppermute | solution.py:39
  279.1 63.2 %all-to-all-start = ((s32[1,16,1]{2,0,1:T(1,128)}), s32[1,16,1]{2,0,1:T(1,128)S(1)}, u32[]{:S(2)}, u32[]{:S(2)}) async-start(s32[1,16,1]{2,0,1:T(1,128)} %copy.32), calls=%async_computation | async-start | bytes 16384 | tf_op jit(solution)/shard_map/all_to_all | solution.py:62
  298.5 15.4 %collective-permute-start.17 = (bf16[384,1024]{0,1:T(8,128)(2,1)}, bf16[384,1024]{0,1:T(8,128)(2,1)}, u32[]{:S(2)}, u32[]{:S(2)}) collective-permute-start(bf16[384,1024]{0,1:T(8,128)(2,1)} %collective-permute-done.16), channel_id=1, source_target_pairs={{0,1},{1,2},{2,3},{3,4},{4,5},{5,6},{6,7},{7,8},{8,9},{9,10},{10,1... | collective-permute-start | bytes 2359304 | tf_op jit(solution)/shard_map/ppermute | solution.py:39
  342.3 84.5 %all-to-all-start.1 = ((bf16[384,16,128]{2,0,1:T(8,128)(2,1)}), bf16[384,16,128]{2,0,1:T(8,128)(2,1)S(1)}, u32[]{:S(2)}, u32[]{:S(2)}) async-start(bf16[384,16,128]{2,0,1:T(8,128)(2,1)} %fusion.8), calls=%async_computation.1 | async-start | bytes 3145728 | tf_op jit(solution)/shard_map/all_to_all | solution.py:61
  352.6 163.2 %reduce-scatter.4.cloned.1.call-start = ((), (), s32[]{:S(2)}) async-start(), calls=%async_computation.3 | async-start | bytes 1114112
  388.3 127.5 %copy-start.1 = (bf16[1,16,128,128]{3,2,1,0:T(8,128)(2,1)S(1)}, bf16[1,16,128,128]{3,2,1,0:T(8,128)(2,1)}, u32[]{:S(2)}) copy-start(bf16[1,16,128,128]{3,2,1,0:T(8,128)(2,1)} %param.11) | copy-start | bytes 1572868
  398.9 30.8 %copy-start.15 = (s32[1,1,12]{2,1,0:T(1,128)S(1)}, s32[1,1,12]{2,1,0:T(1,128)}, u32[]{:S(2)}) copy-start(s32[1,1,12]{2,1,0:T(1,128)} %param.16) | copy-start | bytes 148
  427.8 8.2 %collective-permute-start.1 = (bf16[384,8,128]{2,1,0:T(8,128)(2,1)S(1)}, bf16[384,8,128]{2,1,0:T(8,128)(2,1)S(1)}, u32[]{:S(2)}, u32[]{:S(2)}) collective-permute-start(bf16[384,8,128]{2,1,0:T(8,128)(2,1)S(1)} %fusion.24), channel_id=1, source_target_pairs={{0,256},{256,0},{1,257},{257,1},{2,258},{258,2},{3,259},{259,3},{4... | collective-permute-start | bytes 2359304 | tf_op jit(solution)/shard_map/ppermute | solution.py:9
  429.7 6.2 %collective-permute-start.2 = (s32[12]{0:T(128)S(1)}, s32[12]{0:T(128)S(1)}, u32[]{:S(2)}, u32[]{:S(2)}) collective-permute-start(s32[12]{0:T(128)S(1)} %bitcast.72), channel_id=1, source_target_pairs={{0,256},{256,0},{1,257},{257,1},{2,258},{258,2},{3,259},{259,3},{4... | collective-permute-start | bytes 152 | tf_op jit(solution)/shard_map/ppermute | solution.py:9
  432.1 3.1 collective-permute-start
Sparse Core Ops, SparseCore 0:
  426.5 89.1 reduce-scatter.3
